TPU v7x, 256 devices: a whole 4x4x8 slice. The times are simulated.
256 devices in a mesh: samp: 16 (over y_hi, x, core), par: 16 (over z, y_lo).
Axes of the slice: x: 4, y: 4 (y_hi: 2, y_lo: 2; y = y_hi * 2 + y_lo), z: 8, core: 2. Of those that a mesh axis runs over, the one named last changes fastest.
Arguments:
- log_derivs: float32 [2, 8192, 6144], P(None, 'samp', 'par'), may hold values from -60 to 60, as said below
Outputs:
- gram: float32 [8192, 8192], P('samp', 'par')
Inputs may be any that keep to these rules, and one draw needn't show every extreme that they name: `log_derivs`: finite log-derivatives.
All inputs are finite; a program needn't handle non-finite values.
Results may differ from a plain program's by a relative error of at most 0.0001.
Values sent between devices are 32-bit elements; how exact they have to be, the bound alone decides.
A program may use at most 128 MiB of HBM per device.

v0:
```python
import jax
import jax.numpy as jnp
from jax import lax
from jax.sharding import PartitionSpec as P


def tile_product(own_rows, panel):
    tile_block = jnp.dot(
        own_rows, panel.T, precision=lax.Precision.HIGHEST, preferred_element_type=jnp.float32
    )
    return tile_block


def shards(log_derivs):
    slab_count, own_count, param_count = log_derivs.shape
    sample_total = own_count * lax.axis_size("samp")
    scale = 1.0 / (slab_count * param_count * lax.axis_size("par"))
    col_mean = lax.psum(jnp.sum(log_derivs, axis=1), "samp") / sample_total
    sent = log_derivs - col_mean[:, None, :]
    panel = lax.all_gather(sent, "samp", axis=1, tiled=True)
    tile_sum = tile_product(sent[0], panel[0])
    tile_sum = tile_sum + tile_product(sent[1], panel[1])
    result = lax.psum_scatter(tile_sum, "par", scatter_dimension=1, tiled=True)
    return result * scale


def solution(mesh):
    in_specs = (P(None, "samp", "par"),)
    out_specs = P("samp", "par")
    return jax.shard_map(shards, mesh=mesh, in_specs=in_specs, out_specs=out_specs, check_vma=False)
```

profile of v0, /device:TPU:1, one launch (start us, length us, event | category | flops | bytes accessed | tf_op | source)
XLA Modules:
  0.0 622.2 jit_solution(12971258217929908869)
XLA Ops:
  6.5 0.0 all-gather.2.cloned.1.call-start
  6.5 1.5 reduce_sum.9
  8.1 35.7 %psum.7 = f32[2,384]{1,0:T(2,128)S(1)} all-reduce(f32[2,384]{1,0:T(2,128)S(1)} %reduce_sum.9), channel_id=1, replica_groups=mesh['samp'=16,'par'=16] {'samp'}, use_global_device_ids=true, to_apply=%region_1.0 | all-reduce | flops 768 | bytes 6144 | tf_op jit(solution)/shard_map/psum | solution.py:18
  43.8 2.7 broadcast_subtract_fusion
  46.6 0.0 all-gather.2.cloned.1.call-update
  46.6 0.0 copy-start
  46.6 0.0 reduce-scatter.2.cloned.1.call-start
  46.6 156.0 %all-gather.2.cloned.1.call-done = f32[2,8192,384]{2,1,0:T(8,128)} async-done(((f32[2,512,384]{2,1,0:T(8,128)}), f32[2,8192,384]{2,1,0:T(8,128)}) %all-gather.2.cloned.1.call-update) | async-done | bytes 25165840 | tf_op jit(solution)/shard_map/all_gather | solution.py:20
  202.7 29.9 %fusion = f32[512,8192]{1,0:T(8,128)S(1)} fusion(f32[2,8192,384]{2,1,0:T(8,128)} %all-gather.2.cloned.1.call-done, f32[2,512,384]{2,1,0:T(8,128)} %broadcast_subtract_fusion), kind=kOutput, calls=%fused_computation.3 | convolution fusion | flops 19327352832 | bytes 30146560 | tf_op jit(solution)/shard_map/dot_general | solution.py:8
  232.6 0.0 copy-done
  232.6 31.4 %convolution_add_fusion = f32[512,8192]{1,0:T(8,128)} fusion(f32[512,8192]{1,0:T(8,128)S(1)} %fusion, f32[2,8192,384]{2,1,0:T(8,128)} %all-gather.2.cloned.1.call-done, f32[2,512,384]{2,1,0:T(8,128)S(1)} %copy-done), kind=kOutput, calls=%fused_computation | convolution fusion | flops 19331547136 | bytes 46923776 | tf_op jit(solution)/shard_map/dot_general | solution.py:8
  264.0 0.0 reduce-scatter.2.cloned.1.call-update
  264.0 349.0 %reduce-scatter.2.cloned.1.call-done = f32[512,512]{1,0:T(8,128)} async-done(((f32[512,8192]{1,0:T(8,128)}), f32[512,512]{1,0:T(8,128)}) %reduce-scatter.2.cloned.1.call-update) | async-done | bytes 1048592 | tf_op jit(solution)/shard_map/reduce_scatter | solution.py:23
  613.0 2.3 broadcast_multiply_fusion
  (1 shorter events, 0.0 us)
Async XLA Ops:
  6.5 196.1 %all-gather.2.cloned.1.call-start = ((), (), s32[]{:S(2)}) async-start(), calls=%async_computation.1 | async-start | bytes 26738688 | tf_op jit(solution)/shard_map/all_gather | solution.py:20
  46.6 186.0 %copy-start = (f32[2,512,384]{2,1,0:T(8,128)S(1)}, f32[2,512,384]{2,1,0:T(8,128)}, u32[]{:S(2)}) copy-start(f32[2,512,384]{2,1,0:T(8,128)} %broadcast_subtract_fusion) | copy-start | bytes 4718596
  46.6 566.4 %reduce-scatter.2.cloned.1.call-start = ((), (), s32[]{:S(2)}) async-start(), calls=%async_computation.2 | async-start | bytes 17825792 | tf_op jit(solution)/shard_map/reduce_scatter | solution.py:23
Sparse Core Ops, SparseCore 0:
  46.7 155.9 all-gather.1
  264.2 348.8 reduce-scatter.1
where the time goes:
time: 622 us
  waiting for transfers between devices  505 us (81%)
  matrix products  61.3 us (10%)
  blocking collectives  35.7 us (6%)
  between operations  13.4 us (2%)
  other arithmetic  6.59 us (1%)
    reduce_scatter x1, waiting for transfers between devices, shards(): result = lax.psum_scatter(tile_sum, 'par', scatter_dimension=1, tiled=True)  349 us
    all_gather x1, waiting for transfers between devices, shards(): panel = lax.all_gather(sent, 'samp', axis=1, tiled=True)  156 us
    dot_general x2, matrix products, tile_product(): jnp.dot(own_rows, panel.T, precision=lax.Precision.HIGHEST, preferred_ele...  61.3 us
    psum x1, blocking collectives, shards(): col_mean = lax.psum(jnp.sum(log_derivs, axis=1), 'samp') / sample_total  35.7 us
  transfers between devices with their start and end apart: 2, of which 2 were waited for; matrix products, arithmetic and copies ran while one was open for 0% of the time, Pallas kernels for 0%

commit v1 on v0

v1 whole, which is shorter than its diff:
```python
import functools

import jax
import jax.numpy as jnp
from jax import lax
from jax.experimental import pallas as pl
from jax.experimental.pallas import tpu as pltpu
from jax.sharding import PartitionSpec as P

MESH = pl.DeviceIdType.MESH
NX, NY, NZ = 4, 4, 8
UNIT = 512
HALF = UNIT // 2
PART = 384
KU = 2 * PART
N = 4
CH = HALF // N
SAMPLES = 8192
SCALE = 1.0 / 12288.0

ONCE = ["sib0", "sib1", "m1a", "m1b", "m1c", "m2a", "m2b", "m2c", "row0", "row1"]
EACH = [
    "oa", "ob", "j0", "xr", "xl", "fr", "fl", "j1", "j2", "j3", "g0", "g1", "g2", "g3",
    "z0p", "z0m", "z1p", "z1m", "z2p", "z2m", "z3p", "z3m", "fin",
]
SEMS = len(ONCE) + N * len(EACH)


def slot(kind, q=None):
    return ONCE.index(kind) if q is None else len(ONCE) + q * len(EACH) + EACH.index(kind)


def split(value):
    hi = value.astype(jnp.bfloat16)
    return hi, (value - hi.astype(jnp.float32)).astype(jnp.bfloat16)


def kernel(
    in_ref, out_ref,
    raw, rhi, rlo, cols, chi, clo, relay_a, relay_b, tile, zhalf, zfull, fin_out, fin,
    msum, m1, m2, mean, send_sem, recv_sem,
):
    samp, par = lax.axis_index("samp"), lax.axis_index("par")
    core, x, yhi = lax.rem(samp, 2), lax.rem(lax.div(samp, 2), NX), lax.div(samp, 2 * NX)
    z, ylo = lax.div(par, 2), lax.rem(par, 2)
    y = 2 * yhi + ylo
    other = 1 - core
    yb = y + 1 - 2 * ylo
    yo = lax.rem(y + 3 + 2 * ylo, NY)
    yd = lax.rem(y + 2, NY)
    xp, xm, xd = (lax.rem(x + d, NX) for d in (1, 3, 2))
    zp, zm = lax.rem(z + 1, NZ), lax.rem(z + NZ - 1, NZ)

    def dev(x=x, y=y, z=z, core=core):
        return (lax.div(y, 2) * (2 * NX) + x * 2 + core, z * 2 + lax.rem(y, 2))

    sib = dev(core=other)
    to_yb, to_yo, to_yd = dev(y=yb), dev(y=yo), dev(y=yd)
    to_xp, to_xm, to_xd = dev(x=xp), dev(x=xm), dev(x=xd)
    to_zp, to_zm = dev(z=zp), dev(z=zm)

    sent = []

    def copy(kind, q, src, dst, to):
        i = slot(kind, q)
        return pltpu.make_async_remote_copy(
            src_ref=src, dst_ref=dst, send_sem=send_sem.at[i], recv_sem=recv_sem.at[i], device_id=to, device_id_type=MESH
        )

    def send(kind, q, src, dst, to):
        c = copy(kind, q, src, dst, to)
        c.start()
        sent.append(c)

    def arrived(kind, q, ref):
        copy(kind, q, ref, ref, sib).wait_recv()

    barrier = pltpu.get_barrier_semaphore()
    peers = (sib, to_yb, to_yo, to_yd, to_xp, to_xm, to_xd, to_zp, to_zm)
    for peer in peers:
        pl.semaphore_signal(barrier, inc=1, device_id=peer, device_id_type=MESH)

    def at(start, size):
        return pl.ds(pl.multiple_of(start, 8), size)

    msum[...] = jnp.zeros_like(msum)

    @pl.loop(0, 8)
    def _(i):
        acc = msum[0]
        rows = at(core * UNIT + i * 64, 64)
        for s in range(2):
            part = in_ref[s, at(i * 64, 64), :]
            raw[ylo, rows, s * PART:(s + 1) * PART] = part
            msum[0, :, s * PART:(s + 1) * PART] = acc[:, s * PART:(s + 1) * PART] + jnp.sum(part.reshape(8, 8, PART), axis=0)

    pl.semaphore_wait(barrier, len(peers))

    def exchange(kind, half):
        rows = at(core * UNIT + half * HALF, HALF)
        send(kind, None, raw.at[ylo, rows], raw.at[ylo, rows], sib)

    exchange("sib0", other)
    exchange("sib1", core)
    arrived("sib0", None, raw.at[ylo, at(other * UNIT + core * HALF, HALF)])

    def chunk_rows(colour, q):
        return at(colour * UNIT + core * HALF + q * CH, CH)

    def piece(x, rel, q):
        return cols.at[q, x, at(rel * CH, CH)]

    def send_y(q):
        away = raw.at[ylo, chunk_rows(1 - ylo, q)]
        send("oa", q, away, piece(x, 2 * ylo, q), to_yb)
        send("ob", q, away, piece(x, 2 - 2 * ylo, q), to_yo)
        rows = raw.at[ylo, chunk_rows(ylo, q)]
        send("j0", q, rows, rows, to_yb)

    send_y(0)
    arrived("sib1", None, raw.at[ylo, at(other * UNIT + other * HALF, HALF)])

    @pl.loop(0, 8)
    def _(i):
        part = raw[ylo, at(other * UNIT + i * 64, 64), :]
        msum[0] = msum[0] + jnp.sum(part.reshape(8, 8, KU), axis=0)

    send("m1a", None, msum.at[0], m1.at[0], to_yb)
    send("m1b", None, msum.at[0], m1.at[1], to_yo)
    send("m1c", None, msum.at[0], m1.at[2], to_yd)
    for q in range(1, N):
        send_y(q)
    for i, kind in enumerate(("m1a", "m1b", "m1c")):
        arrived(kind, None, m1.at[i])
    m2[0, ylo] = msum[0] + m1[2]
    m2[0, 1 - ylo] = m1[0] + m1[1]
    send("m2a", None, m2.at[0], m2.at[1], to_xp)
    send("m2b", None, m2.at[0], m2.at[2], to_xm)
    send("m2c", None, m2.at[0], m2.at[3], to_xd)

    def send_x(q):
        arrived("oa", q, piece(x, 2 - 2 * ylo, q))
        arrived("ob", q, piece(x, 2 * ylo, q))
        cols[q, x, CH:2 * CH, :] = raw[ylo, chunk_rows(ylo, q), :]
        own = cols.at[q, x, 0:3 * CH]
        send("xr", q, own, own, to_xp)
        send("xl", q, own, own, to_xm)
        raw[1 - ylo, chunk_rows(ylo, q), :] = cols[q, x, at((2 - 2 * ylo) * CH, CH), :]
        passed = raw.at[1 - ylo, chunk_rows(1 - ylo, q)]
        arrived("j0", q, passed)
        send("g0", q, passed, piece(x, 3, q), to_yo)

    cut = 3 * CH // 2

    def forward_x(q):
        arrived("xr", q, cols.at[q, xm, 0:3 * CH])
        low = cols.at[q, xm, 0:cut]
        send("fr", q, low, low, to_xp)
        arrived("xl", q, cols.at[q, xp, 0:3 * CH])
        high = cols.at[q, xp, cut:3 * CH]
        send("fl", q, high, high, to_xm)
        send("j1", q, piece(xm, 1, q), relay_b.at[q, 0], to_yo)
        send("j2", q, piece(xp, 1, q), relay_b.at[q, 1], to_yo)

    def end_x(q):
        arrived("fr", q, cols.at[q, xd, 0:cut])
        arrived("fl", q, cols.at[q, xd, cut:3 * CH])
        send("j3", q, piece(xd, 1, q), relay_a.at[q], to_yb)

    def relays(q):
        arrived("j1", q, relay_b.at[q, 0])
        send("g1", q, relay_b.at[q, 0], piece(xm, 3, q), to_yb)
        arrived("j2", q, relay_b.at[q, 1])
        send("g2", q, relay_b.at[q, 1], piece(xp, 3, q), to_yb)
        arrived("j3", q, relay_a.at[q])
        send("g3", q, relay_a.at[q], piece(xd, 3, q), to_yo)

    def rows_ready():
        for c in range(2):
            rows = at(c * UNIT + core * HALF, HALF)
            send(f"row{c}", None, raw.at[1 - ylo, rows], raw.at[1 - ylo, rows], sib)
        for i, kind in enumerate(("m2a", "m2b", "m2c")):
            arrived(kind, None, m2.at[i + 1])
        total = (m2[0] + m2[1]) + (m2[2] + m2[3])
        mean[...] = jnp.sum(total, axis=1, keepdims=True) / SAMPLES
        for c in range(2):
            arrived(f"row{c}", None, raw.at[1 - ylo, at(c * UNIT + other * HALF, HALF)])

        @pl.loop(0, 16)
        def _(i):
            rows = at(i * 64, 64)
            for p in range(2):
                hi, lo = split(raw[p, rows, :] - mean[p])
                rhi[rows, p * KU:(p + 1) * KU] = hi
                rlo[rows, p * KU:(p + 1) * KU] = lo

    def product(q):
        arrived("g0", q, piece(x, 3, q))
        arrived("g1", q, piece(xm, 3, q))
        arrived("g2", q, piece(xp, 3, q))
        arrived("g3", q, piece(xd, 3, q))

        @pl.loop(0, 8)
        def _(s):
            to = pl.ds(pl.multiple_of(s * CH, CH), CH)
            for p in range(2):
                rel = lax.rem(2 * lax.div(s, NX) + p - y + 5, NY)
                value = cols[q, lax.rem(s, NX), at(rel * CH, CH), :]
                hi, lo = split(value - mean[p])
                chi[to, p * KU:(p + 1) * KU] = hi
                clo[to, p * KU:(p + 1) * KU] = lo

        dims = (((1,), (1,)), ((), ()))
        dot = functools.partial(lax.dot_general, dimension_numbers=dims, preferred_element_type=jnp.float32)

        @pl.loop(0, 4)
        def _(r):
            lanes = pl.ds(pl.multiple_of(r * 256, 256), 256)
            ch, rh = chi[...], rhi[lanes, :]
            tile[q, :, lanes] = dot(ch, rh) + dot(ch, rlo[lanes, :]) + dot(clo[...], rh)

    def block(q, step):
        return at(lax.rem(z + step + NZ, NZ) * CH, CH)

    def reduce0(q):
        rows = block(q, 4)
        send("z0p", q, tile.at[q, rows, UNIT:2 * UNIT], zhalf.at[q, 0], to_zp)
        send("z0m", q, tile.at[q, rows, 0:UNIT], zhalf.at[q, 1], to_zm)

    def reduce1(q):
        for d, kind, nxt, to, lanes, step in (
            (0, "z0p", "z1p", to_zp, slice(UNIT, 2 * UNIT), 3), (1, "z0m", "z1m", to_zm, slice(0, UNIT), -3),
        ):
            arrived(kind, q, zhalf.at[q, d])
            rows = block(q, step)
            tile[q, rows, lanes] = tile[q, rows, lanes] + zhalf[q, d]
            send(nxt, q, tile.at[q, rows], zfull.at[q, d, 0], to)

    def reduce_mid(q, i):
        for d, tag, to, step in ((0, "p", to_zp, 3 - i), (1, "m", to_zm, i - 3)):
            arrived(f"z{i}{tag}", q, zfull.at[q, d, i - 1])
            rows = block(q, step)
            tile[q, rows, :] = tile[q, rows, :] + zfull[q, d, i - 1]
            send(f"z{i + 1}{tag}", q, tile.at[q, rows], zfull.at[q, d, i], to)

    def reduce_end(q):
        arrived("z3p", q, zfull.at[q, 0, 2])
        arrived("z3m", q, zfull.at[q, 1, 2])
        total = (tile[q, block(q, 0), :] + (zfull[q, 0, 2] + zfull[q, 1, 2])) * SCALE
        low, high = total[:, :UNIT], total[:, UNIT:]
        first = core == 0
        fin[at(core * HALF + q * CH, CH), :] = jnp.where(first, low, high)
        fin_out[q] = jnp.where(first, high, low)
        send("fin", q, fin_out.at[q], fin.at[at(core * HALF + q * CH, CH)], sib)

    send_x(0)
    send_x(1)
    forward_x(0)
    send_x(2)
    end_x(0)
    send_x(3)
    rows_ready()
    relays(0)
    forward_x(1)
    product(0)
    reduce0(0)
    end_x(1)
    forward_x(2)
    relays(1)
    reduce1(0)
    product(1)
    reduce0(1)
    reduce_mid(0, 1)
    end_x(2)
    forward_x(3)
    relays(2)
    reduce1(1)
    reduce_mid(0, 2)
    product(2)
    reduce0(2)
    reduce_mid(1, 1)
    end_x(3)
    reduce_end(0)
    relays(3)
    reduce1(2)
    reduce_mid(1, 2)
    product(3)
    reduce0(3)
    reduce_mid(2, 1)
    reduce_end(1)
    reduce1(3)
    reduce_mid(2, 2)
    reduce_mid(3, 1)
    reduce_end(2)
    reduce_mid(3, 2)
    reduce_end(3)
    for q in range(N):
        arrived("fin", q, fin.at[at(other * HALF + q * CH, CH)])
    out_ref[...] = fin[...].T
    for c in sent:
        c.wait_send()


def shards(log_derivs):
    f32, bf16, VMEM = jnp.float32, jnp.bfloat16, pltpu.VMEM
    rows, depth, width = 2 * UNIT, 2 * KU, 8 * CH
    scratch = [
        VMEM((2, rows, KU), f32), VMEM((rows, depth), bf16), VMEM((rows, depth), bf16),
        VMEM((N, NX, 4 * CH, KU), f32), VMEM((width, depth), bf16), VMEM((width, depth), bf16),
        VMEM((N, CH, KU), f32), VMEM((N, 2, CH, KU), f32),
        VMEM((N, width, rows), f32), VMEM((N, 2, CH, UNIT), f32), VMEM((N, 2, 3, CH, rows), f32),
        VMEM((N, CH, UNIT), f32), VMEM((UNIT, UNIT), f32),
        VMEM((1, 8, KU), f32), VMEM((3, 8, KU), f32), VMEM((4, 2, 8, KU), f32), VMEM((2, 1, KU), f32),
        pltpu.SemaphoreType.DMA((SEMS,)), pltpu.SemaphoreType.DMA((SEMS,)),
    ]
    return pl.pallas_call(
        kernel,
        out_shape=jax.ShapeDtypeStruct((UNIT, UNIT), f32),
        in_specs=[pl.BlockSpec(memory_space=VMEM)],
        out_specs=pl.BlockSpec(memory_space=VMEM),
        scratch_shapes=scratch,
        compiler_params=pltpu.CompilerParams(collective_id=0, has_side_effects=True, vmem_limit_bytes=60 * 2**20),
        cost_estimate=pl.CostEstimate(flops=20 * 10**9, bytes_accessed=4 * 2**20, transcendentals=0),
    )(log_derivs)


def solution(mesh):
    in_specs = (P(None, "samp", "par"),)
    out_specs = P("samp", "par")
    return jax.shard_map(shards, mesh=mesh, in_specs=in_specs, out_specs=out_specs, check_vma=False)
```

time: 622 us -> 193 us (0.31)
  waiting for transfers between devices: 505 us -> 0 us
  Pallas kernels: 0 us -> 191 us
  matrix products: 61.3 us -> 0 us
  blocking collectives: 35.7 us -> 0 us
  between operations: 13.4 us -> 0.01 us
  other arithmetic: 6.59 us -> 0 us
    reduce_scatter x1 -> x0, waiting for transfers between devices: 349 us -> none  [shards(): result = lax.psum_scatter(tile_sum, 'par', scatter_dimension=1, tiled=True)]
    pallas_call x0 -> x1, Pallas kernels: none -> 191 us  [shards(): pl.pallas_call(kernel, out_shape=jax.ShapeDtypeStruct((UNIT, UNIT), f32),...]
    all_gather x1 -> x0, waiting for transfers between devices: 156 us -> none  [shards(): panel = lax.all_gather(sent, 'samp', axis=1, tiled=True)]
    dot_general x2 -> x0, matrix products: 61.3 us -> none  [tile_product(): jnp.dot(own_rows, panel.T, precision=lax.Precision.HIGHEST, preferred_ele...]
    psum x1 -> x0, blocking collectives: 35.7 us -> none  [shards(): col_mean = lax.psum(jnp.sum(log_derivs, axis=1), 'samp') / sample_total]
  transfers between devices with their start and end apart: 2 -> 0, of which waited for: 2 -> 0; matrix products, arithmetic and copies ran while one was open for 0% -> 0% of each run, Pallas kernels for 0% -> 0%
where the time goes in v1:
time: 193 us
  Pallas kernels  191 us (99%)
  local copies, waits for them, and re-layouts  2.26 us (1%)
    pallas_call x1, Pallas kernels, shards(): pl.pallas_call(kernel, out_shape=jax.ShapeDtypeStruct((UNIT, UNIT), f32),...  191 us

profile of v1, /device:TPU:1, one launch (start us, length us, event | category | flops | bytes accessed | tf_op | source)
XLA Modules:
  0.0 193.3 jit_solution(4287200139813080292)
XLA Ops:
  0.0 191.0 %shard_map.17 = f32[512,512]{1,0:T(8,128)} custom-call(f32[2,512,384]{2,1,0:T(8,128)} %in_ref.1), custom_call_target="tpu_custom_call" | custom-call | flops 20000000000 | bytes 4194304 | tf_op jit(solution)/shard_map/pallas_call | solution.py:316
  191.0 2.3 %copy.3 = f32[512,512]{1,0:T(8,128)} copy(f32[512,512]{1,0:T(8,128)} %shard_map.17) | data formatting | bytes 2097152

commit v2 on v0

v2 whole, which is shorter than its diff:
```python
import functools

import jax
import jax.numpy as jnp
from jax import lax
from jax.experimental import pallas as pl
from jax.experimental.pallas import tpu as pltpu
from jax.sharding import PartitionSpec as P

MESH = pl.DeviceIdType.MESH
NX, NY, NZ = 4, 4, 8
UNIT = 512
HALF = UNIT // 2
PART = 384
KEEP = 3
KU = 2 * PART
SIZES = (32, 32, 32, 32, 32, 32, 32, 32)
N = len(SIZES)
START = tuple(sum(SIZES[:q]) for q in range(N))
SAMPLES = 8192
SCALE = 1.0 / 12288.0
ACROSS = (False, False, True, True, True, True, True, True)
GROUP = 64
GROUPS = HALF // GROUP
PARTS = (
    (0, 0, 1), (0, 1, 1), (1, 0, 2), (0, 2, 1), (1, 2, 1), (0, 3, 1), (1, 3, 1), (2, 0, 4), (3, 0, 4), (4, 0, 4),
    (5, 0, 4), (6, 0, 4), (7, 0, 2), (7, 2, 2),
)

ONCE = ["sib0", "sib1", "m1a", "m1b", "m1c", "m2a", "m2b", "m2c"] + [f"row{i}" for i in range(2 * GROUPS)]
EACH = [
    "oa", "ob", "j0", "g0", "xr0", "xl0", "fr0", "fl0", "xr1", "xl1", "fr1", "fl1", "xr2", "xl2", "fr2", "fl2",
]
REDUCE = ["z0p", "z0m", "z1p", "z1m", "z2p", "z2m", "z3p", "z3m", "fin"]
SEMS = len(ONCE) + N * len(EACH) + len(PARTS) * len(REDUCE)

ORDER = (
    (3, 0), (4, 0), (5, 0), (5, 2), (4, 1), (0, 0), (3, 1), (3, 2), (3, 3), (6, 0), (8, 0), (7, 0), (10, 2), (4, 3),
    (3, 4), (4, 5), (3, 5), (3, 6), (3, 7), (10, 0), (1, 0), (6, 1), (9, 0), (5, 1), (11, 0), (7, 1), (2, 0), (12,
    0), (7, 2), (4, 7), (13, 0), (9, 1), (8, 1), (6, 2), (6, 3), (4, 6), (12, 2), (4, 2), (4, 4), (10, 1), (14, 2),
    (15, 2), (5, 3), (7, 3), (2, 1), (13, 1), (6, 4), (16, 0), (17, 0), (17, 1), (18, 0), (6, 5), (18, 1), (11, 1),
    (7, 4), (7, 5), (2, 2), (19, 0), (5, 4), (8, 2), (19, 1), (12, 1), (16, 1), (17, 2), (18, 2), (10, 3), (14, 3),
    (17, 3), (18, 3), (17, 4), (18, 4), (6, 7), (20, 0), (19, 2), (6, 6), (8, 3), (7, 7), (7, 6), (2, 3), (17, 5),
    (18, 5), (20, 2), (12, 3), (15, 3), (11, 2), (19, 4), (19, 3), (8, 4), (17, 6), (18, 6), (19, 5), (20, 1), (10,
    4), (21, 2), (9, 3), (14, 4), (21, 0), (20, 4), (9, 2), (11, 3), (20, 3), (19, 6), (16, 2), (17, 7), (18, 7),
    (20, 5), (5, 5), (8, 5), (21, 1), (21, 4), (16, 3), (20, 6), (19, 7), (17, 8), (18, 8), (12, 4), (15, 4), (11,
    4), (5, 6), (21, 5), (21, 3), (21, 6), (10, 5), (20, 7), (14, 5), (19, 8), (8, 6), (9, 4), (16, 4), (17, 9),
    (18, 9), (10, 6), (12, 5), (15, 5), (21, 7), (22, 4), (9, 6), (11, 5), (5, 7), (22, 5), (19, 9), (12, 6), (15,
    6), (20, 8), (22, 1), (22, 0), (8, 7), (9, 5), (16, 5), (14, 6), (10, 7), (14, 7), (11, 6), (20, 9), (17, 10),
    (18, 10), (21, 8), (12, 7), (15, 7), (11, 7), (22, 6), (21, 9), (16, 6), (17, 11), (18, 11), (19, 10), (9, 7),
    (16, 7), (17, 12), (18, 12), (19, 11), (20, 10), (19, 12), (22, 2), (17, 13), (18, 13), (22, 3), (20, 11), (20,
    12), (19, 13), (22, 8), (22, 9), (21, 10), (20, 13), (21, 12), (21, 11), (21, 13), (22, 7), (22, 12), (22, 10),
    (22, 11), (22, 13),
)


def slot(kind, q=None):
    if q is None:
        return ONCE.index(kind)
    if kind in REDUCE:
        return len(ONCE) + N * len(EACH) + q * len(REDUCE) + REDUCE.index(kind)
    return len(ONCE) + q * len(EACH) + EACH.index(kind)


def split(value):
    hi = value.astype(jnp.bfloat16)
    return hi, (value - hi.astype(jnp.float32)).astype(jnp.bfloat16)


def kernel(
    in_ref, out_ref,
    raw, rhi, rlo, cols, chi, clo, tile, zhalf, zfull, fin_out, fin,
    msum, m1, m2, mean, send_sem, recv_sem,
):
    samp, par = lax.axis_index("samp"), lax.axis_index("par")
    core, x, yhi = lax.rem(samp, 2), lax.rem(lax.div(samp, 2), NX), lax.div(samp, 2 * NX)
    z, ylo = lax.div(par, 2), lax.rem(par, 2)
    y = 2 * yhi + ylo
    other = 1 - core
    yb = y + 1 - 2 * ylo
    yo = lax.rem(y + 3 + 2 * ylo, NY)
    yd = lax.rem(y + 2, NY)
    xp, xm, xd = (lax.rem(x + d, NX) for d in (1, 3, 2))
    zp, zm = lax.rem(z + 1, NZ), lax.rem(z + NZ - 1, NZ)

    def dev(x=x, y=y, z=z, core=core):
        return (lax.div(y, 2) * (2 * NX) + x * 2 + core, z * 2 + lax.rem(y, 2))

    sib = dev(core=other)
    to_yb, to_yo, to_yd = dev(y=yb), dev(y=yo), dev(y=yd)
    to_xp, to_xm, to_xd = dev(x=xp), dev(x=xm), dev(x=xd)
    to_zp, to_zm = dev(z=zp), dev(z=zm)

    sent = []

    def copy(kind, q, src, dst, to):
        i = slot(kind, q)
        return pltpu.make_async_remote_copy(
            src_ref=src, dst_ref=dst, send_sem=send_sem.at[i], recv_sem=recv_sem.at[i], device_id=to, device_id_type=MESH
        )

    def send(kind, q, src, dst, to):
        c = copy(kind, q, src, dst, to)
        c.start()
        sent.append(c)

    def arrived(kind, q, ref):
        copy(kind, q, ref, ref, sib).wait_recv()

    barrier = pltpu.get_barrier_semaphore()
    peers = (sib, to_yb, to_yo, to_yd, to_xp, to_xm, to_xd, to_zp, to_zm)
    for peer in peers:
        pl.semaphore_signal(barrier, inc=1, device_id=peer, device_id_type=MESH)

    def at(start, size):
        return pl.ds(pl.multiple_of(start, 8), size)

    def chunk_rows(colour, q):
        return at(colour * UNIT + core * HALF + START[q], SIZES[q])

    def piece(x, rel, q, size=1):
        return cols.at[x, at(4 * START[q] + rel * SIZES[q], size * SIZES[q])]

    def send_yo(q):
        send("ob", q, raw.at[ylo, chunk_rows(1 - ylo, q)], piece(x, 1 - ylo, q), to_yo)

    def send_yb(q):
        send("oa", q, raw.at[ylo, chunk_rows(1 - ylo, q)], piece(x, ylo, q), to_yb)
        rows = raw.at[ylo, chunk_rows(ylo, q)]
        send("j0", q, rows, rows, to_yb)

    def send_own(q):
        own = piece(x, 2, q)
        own[...] = raw[ylo, chunk_rows(ylo, q), :]
        send("xr0", q, own, own, to_xp)
        send("xl0", q, own, own, to_xm)

    def recv_next(q):
        arrived("oa", q, piece(x, 1 - ylo, q))
        raw[1 - ylo, chunk_rows(ylo, q), :] = piece(x, 1 - ylo, q)[...]

    def send_next(q):
        arrived("ob", q, piece(x, ylo, q))
        both = piece(x, 0, q, 2)
        send("xr1", q, both, both, to_xp)
        send("xl1", q, both, both, to_xm)

    def pass_far(q):
        passed = raw.at[1 - ylo, chunk_rows(1 - ylo, q)]
        arrived("j0", q, passed)
        send("g0", q, passed, piece(x, 3, q), to_yo)

    def send_far(q):
        arrived("g0", q, piece(x, 3, q))
        if not ACROSS[q]:
            far = piece(x, 3, q)
            send("xr2", q, far, far, to_xp)
            send("xl2", q, far, far, to_xm)

    def halves(rel, x, q):
        h = SIZES[q] // 2
        first = 4 * START[q] + rel * SIZES[q]
        return cols.at[x, at(first, h)], cols.at[x, at(first + h, h)]

    def forward_one(i, rel, q):
        arrived(f"xr{i}", q, piece(xm, rel, q))
        low = halves(rel, xm, q)[0]
        send(f"fr{i}", q, low, low, to_xp)
        arrived(f"xl{i}", q, piece(xp, rel, q))
        high = halves(rel, xp, q)[1]
        send(f"fl{i}", q, high, high, to_xm)

    def end_one(i, rel, q):
        low, high = halves(rel, xd, q)
        arrived(f"fr{i}", q, low)
        arrived(f"fl{i}", q, high)

    def forward_own(q):
        forward_one(0, 2, q)

    def across1(q):
        send("xr2", q, piece(xm, 2, q), piece(xm, 3, q), to_yd)
        send("xl2", q, piece(xp, 2, q), piece(xp, 3, q), to_yd)

    def across2(q):
        send("fr2", q, piece(xd, 2, q), piece(xd, 3, q), to_yd)

    def end_own(q):
        end_one(0, 2, q)

    def forward_next(q):
        arrived("xr1", q, piece(xm, 0, q, 2))
        low = piece(xm, 0, q)
        send("fr1", q, low, low, to_xp)
        arrived("xl1", q, piece(xp, 0, q, 2))
        high = piece(xp, 1, q)
        send("fl1", q, high, high, to_xm)

    def forward_far(q):
        forward_one(2, 3, q)

    def columns_ready(q):
        arrived("fr1", q, piece(xd, 0, q))
        arrived("fl1", q, piece(xd, 1, q))
        if ACROSS[q]:
            arrived("xr2", q, piece(xm, 3, q))
            arrived("xl2", q, piece(xp, 3, q))
            arrived("fr2", q, piece(xd, 3, q))
        else:
            end_one(2, 3, q)

    def send_rows(j):
        for c in range(2):
            rows = at(c * UNIT + core * HALF + j * GROUP, GROUP)
            send(f"row{2 * j + c}", None, raw.at[1 - ylo, rows], raw.at[1 - ylo, rows], sib)

    def rows_ready(j):
        send_rows(j)
        if j == 0:
            for i, kind in enumerate(("m2a", "m2b", "m2c")):
                arrived(kind, None, m2.at[i + 1])
            total = (m2[0] + m2[1]) + (m2[2] + m2[3])
            mean[...] = jnp.sum(total, axis=1, keepdims=True) / SAMPLES
        for c in range(2):
            arrived(f"row{2 * j + c}", None, raw.at[1 - ylo, at(c * UNIT + other * HALF + j * GROUP, GROUP)])

        @pl.loop(0, GROUP // 16)
        def _(i):
            n = GROUP // 64
            src = at(lax.div(i, n) * HALF + j * GROUP + lax.rem(i, n) * 64, 64)
            dst = at(j * 4 * GROUP + i * 64, 64)
            for p in range(2):
                hi, lo = split(raw[p, src, :] - mean[p])
                rhi[dst, p * KU:(p + 1) * KU] = hi
                rlo[dst, p * KU:(p + 1) * KU] = lo

    def columns(q):
        columns_ready(q)
        keep, size = q % KEEP, SIZES[q]

        @pl.loop(0, 8)
        def _(s):
            to = pl.ds(pl.multiple_of(s * size, 16), size)
            for p in range(2):
                off = lax.rem(2 * lax.div(s, NX) + p - y + NY, NY)
                rel = jnp.where(off == 0, 2, jnp.where(off == 1, 1, jnp.where(off == 2, 3, 0)))
                hi, lo = split(piece(lax.rem(s, NX), rel, q)[...] - mean[p])
                chi[keep, to, p * KU:(p + 1) * KU] = hi
                clo[keep, to, p * KU:(p + 1) * KU] = lo

    dims = (((1,), (1,)), ((), ()))
    dot = functools.partial(lax.dot_general, dimension_numbers=dims, preferred_element_type=jnp.float32)

    def product(u):
        q, j0, count = PARTS[u]
        keep, width = q % KEEP, 8 * SIZES[q]

        @pl.loop(0, count * GROUP // 64)
        def _(r):
            rows = pl.ds(pl.multiple_of(j0 * 4 * GROUP + r * HALF, HALF), HALF)
            n = GROUP // 64
            lanes = pl.ds(pl.multiple_of(lax.rem(r, n) * HALF, HALF), HALF)
            ch, rh = chi[keep, :width], rhi[rows, :]
            tile[j0 + lax.div(r, n), 8 * START[q]:8 * START[q] + width, lanes] = (
                dot(ch, rh) + dot(ch, rlo[rows, :]) + dot(clo[keep, :width], rh)
            )

    def block(u, step, lanes=slice(None)):
        q, j0, count = PARTS[u]
        rows = at(8 * START[q] + lax.rem(z + step + NZ, NZ) * SIZES[q], SIZES[q])
        return tile.at[j0:j0 + count, rows, lanes]

    def full(u, d, i):
        q, j0, count = PARTS[u]
        return zfull.at[d, i, j0:j0 + count, START[q]:START[q] + SIZES[q]]

    def half(u, d):
        q, j0, count = PARTS[u]
        return zhalf.at[d, j0:j0 + count, START[q]:START[q] + SIZES[q]]

    low, high = slice(0, 2 * GROUP), slice(2 * GROUP, 4 * GROUP)

    def reduce0(u):
        send("z0p", u, block(u, 4, high), half(u, 0), to_zp)
        send("z0m", u, block(u, 4, low), half(u, 1), to_zm)

    def reduce1(u):
        for d, tag, to, lanes, step in ((0, "p", to_zp, high, 3), (1, "m", to_zm, low, -3)):
            arrived(f"z0{tag}", u, half(u, d))
            part = block(u, step, lanes)
            part[...] = part[...] + half(u, d)[...]
            send(f"z1{tag}", u, block(u, step), full(u, d, 0), to)

    def reduce_mid(u, i):
        for d, tag, to, step in ((0, "p", to_zp, 3 - i), (1, "m", to_zm, i - 3)):
            arrived(f"z{i}{tag}", u, full(u, d, i - 1))
            part = block(u, step)
            part[...] = part[...] + full(u, d, i - 1)[...]
            send(f"z{i + 1}{tag}", u, part, full(u, d, i), to)

    def final(u, c):
        q, j0, count = PARTS[u]
        return fin.at[j0:j0 + count, at(c * HALF + START[q], SIZES[q])]

    def reduce_end(u):
        q, j0, count = PARTS[u]
        arrived("z3p", u, full(u, 0, 2))
        arrived("z3m", u, full(u, 1, 2))
        total = (block(u, 0)[...] + (full(u, 0, 2)[...] + full(u, 1, 2)[...])) * SCALE
        first = core == 0
        final(u, core)[...] = jnp.where(first, total[..., low], total[..., high])
        away = fin_out.at[j0:j0 + count, START[q]:START[q] + SIZES[q]]
        away[...] = jnp.where(first, total[..., high], total[..., low])
        send("fin", u, away, final(u, core), sib)

    def exchange(kind, half):
        rows = at(core * UNIT + half * HALF, HALF)
        send(kind, None, raw.at[ylo, rows], raw.at[ylo, rows], sib)

    def means1():
        arrived("sib1", None, raw.at[ylo, at(other * UNIT + other * HALF, HALF)])
        msum[...] = jnp.zeros_like(msum)

        @pl.loop(0, 16)
        def _(i):
            part = raw[ylo, at(i * 64, 64), :]
            msum[0] = msum[0] + jnp.sum(part.reshape(8, 8, KU), axis=0)

        send("m1a", None, msum.at[0], m1.at[0], to_yb)
        send("m1b", None, msum.at[0], m1.at[1], to_yo)
        send("m1c", None, msum.at[0], m1.at[2], to_yd)

    def means2():
        for i, kind in enumerate(("m1a", "m1b", "m1c")):
            arrived(kind, None, m1.at[i])
        m2[0, ylo] = msum[0] + m1[2]
        m2[0, 1 - ylo] = m1[0] + m1[1]
        send("m2a", None, m2.at[0], m2.at[1], to_xp)
        send("m2b", None, m2.at[0], m2.at[2], to_xm)
        send("m2c", None, m2.at[0], m2.at[3], to_xd)

    @pl.loop(0, 8)
    def _(i):
        for s in range(2):
            raw[ylo, at(core * UNIT + i * 64, 64), s * PART:(s + 1) * PART] = in_ref[s, at(i * 64, 64), :]

    pl.semaphore_wait(barrier, len(peers))
    exchange("sib0", other)
    exchange("sib1", core)
    arrived("sib0", None, raw.at[ylo, at(other * UNIT + core * HALF, HALF)])

    steps = (
        lambda _: means1(), lambda _: means2(), rows_ready,
        send_yb, send_yo, send_own, recv_next, pass_far, send_next, send_far, forward_own, forward_next, end_own,
        forward_far, across1, across2, columns, product, reduce0, reduce1,
        lambda u: reduce_mid(u, 1), lambda u: reduce_mid(u, 2), reduce_end,
    )
    for step, index in ORDER:
        steps[step](index)
    for u in range(len(PARTS)):
        arrived("fin", u, final(u, other))
    for j in range(GROUPS):
        turned = fin[j].T
        for h in range(2):
            out_ref[h * HALF + j * GROUP:h * HALF + (j + 1) * GROUP, :] = turned[h * GROUP:(h + 1) * GROUP]
    for c in sent:
        c.wait_send()


def shards(log_derivs):
    f32, bf16, VMEM = jnp.float32, jnp.bfloat16, pltpu.VMEM
    rows, depth, width = 2 * UNIT, 2 * KU, 8 * max(SIZES)
    scratch = [
        VMEM((2, rows, KU), f32), VMEM((rows, depth), bf16), VMEM((rows, depth), bf16),
        VMEM((NX, 4 * HALF, KU), f32), VMEM((KEEP, width, depth), bf16), VMEM((KEEP, width, depth), bf16),
        VMEM((GROUPS, 8 * HALF, 4 * GROUP), f32),
        VMEM((2, GROUPS, HALF, 2 * GROUP), f32), VMEM((2, 3, GROUPS, HALF, 4 * GROUP), f32),
        VMEM((GROUPS, HALF, 2 * GROUP), f32), VMEM((GROUPS, UNIT, 2 * GROUP), f32),
        VMEM((1, 8, KU), f32), VMEM((3, 8, KU), f32), VMEM((4, 2, 8, KU), f32), VMEM((2, 1, KU), f32),
        pltpu.SemaphoreType.DMA((SEMS,)), pltpu.SemaphoreType.DMA((SEMS,)),
    ]
    return pl.pallas_call(
        kernel,
        out_shape=jax.ShapeDtypeStruct((UNIT, UNIT), f32),
        in_specs=[pl.BlockSpec(memory_space=VMEM)],
        out_specs=pl.BlockSpec(memory_space=VMEM),
        scratch_shapes=scratch,
        compiler_params=pltpu.CompilerParams(collective_id=0, has_side_effects=True, vmem_limit_bytes=60 * 2**20),
        cost_estimate=pl.CostEstimate(flops=20 * 10**9, bytes_accessed=4 * 2**20, transcendentals=0),
    )(log_derivs)


def solution(mesh):
    in_specs = (P(None, "samp", "par"),)
    out_specs = P("samp", "par")
    return jax.shard_map(shards, mesh=mesh, in_specs=in_specs, out_specs=out_specs, check_vma=False)
```

time: 622 us -> 144 us (0.23)
  waiting for transfers between devices: 505 us -> 0 us
  Pallas kernels: 0 us -> 142 us
  matrix products: 61.3 us -> 0 us
  blocking collectives: 35.7 us -> 0 us
  between operations: 13.4 us -> 0.01 us
  other arithmetic: 6.59 us -> 0 us
    reduce_scatter x1 -> x0, waiting for transfers between devices: 349 us -> none  [shards(): result = lax.psum_scatter(tile_sum, 'par', scatter_dimension=1, tiled=True)]
    all_gather x1 -> x0, waiting for transfers between devices: 156 us -> none  [shards(): panel = lax.all_gather(sent, 'samp', axis=1, tiled=True)]
    pallas_call x0 -> x1, Pallas kernels: none -> 142 us  [shards(): pl.pallas_call(kernel, out_shape=jax.ShapeDtypeStruct((UNIT, UNIT), f32),...]
    dot_general x2 -> x0, matrix products: 61.3 us -> none  [tile_product(): jnp.dot(own_rows, panel.T, precision=lax.Precision.HIGHEST, preferred_ele...]
    psum x1 -> x0, blocking collectives: 35.7 us -> none  [shards(): col_mean = lax.psum(jnp.sum(log_derivs, axis=1), 'samp') / sample_total]
  transfers between devices with their start and end apart: 2 -> 0, of which waited for: 2 -> 0; matrix products, arithmetic and copies ran while one was open for 0% -> 0% of each run, Pallas kernels for 0% -> 0%
where the time goes in v2:
time: 144 us
  Pallas kernels  142 us (99%)
  local copies, waits for them, and re-layouts  2.26 us (2%)
    pallas_call x1, Pallas kernels, shards(): pl.pallas_call(kernel, out_shape=jax.ShapeDtypeStruct((UNIT, UNIT), f32),...  142 us

profile of v2, /device:TPU:1, one launch (start us, length us, event | category | flops | bytes accessed | tf_op | source)
XLA Modules:
  0.0 143.9 jit_solution(2883526044692909164)
XLA Ops:
  0.0 141.7 %shard_map.17 = f32[512,512]{1,0:T(8,128)} custom-call(f32[2,512,384]{2,1,0:T(8,128)} %in_ref.1), custom_call_target="tpu_custom_call" | custom-call | flops 20000000000 | bytes 4194304 | tf_op jit(solution)/shard_map/pallas_call | solution.py:382
  141.7 2.3 %copy.3 = f32[512,512]{1,0:T(8,128)} copy(f32[512,512]{1,0:T(8,128)} %shard_map.17) | data formatting | bytes 2097152

commit v3 on v2

--- a/solution.py
+++ b/solution.py
@@ -22,10 +22,13 @@
 ACROSS = (False, False, True, True, True, True, True, True)
 GROUP = 64
 GROUPS = HALF // GROUP
+EARLY = (0,)
 PARTS = (
     (0, 0, 1), (0, 1, 1), (1, 0, 2), (0, 2, 1), (1, 2, 1), (0, 3, 1), (1, 3, 1), (2, 0, 4), (3, 0, 4), (4, 0, 4),
     (5, 0, 4), (6, 0, 4), (7, 0, 2), (7, 2, 2),
 )
+
+LAG = 70
 
 ONCE = ["sib0", "sib1", "m1a", "m1b", "m1c", "m2a", "m2b", "m2c"] + [f"row{i}" for i in range(2 * GROUPS)]
 EACH = [
@@ -35,22 +38,22 @@
 SEMS = len(ONCE) + N * len(EACH) + len(PARTS) * len(REDUCE)
 
 ORDER = (
-    (3, 0), (4, 0), (5, 0), (5, 2), (4, 1), (0, 0), (3, 1), (3, 2), (3, 3), (6, 0), (8, 0), (7, 0), (10, 2), (4, 3),
-    (3, 4), (4, 5), (3, 5), (3, 6), (3, 7), (10, 0), (1, 0), (6, 1), (9, 0), (5, 1), (11, 0), (7, 1), (2, 0), (12,
-    0), (7, 2), (4, 7), (13, 0), (9, 1), (8, 1), (6, 2), (6, 3), (4, 6), (12, 2), (4, 2), (4, 4), (10, 1), (14, 2),
-    (15, 2), (5, 3), (7, 3), (2, 1), (13, 1), (6, 4), (16, 0), (17, 0), (17, 1), (18, 0), (6, 5), (18, 1), (11, 1),
-    (7, 4), (7, 5), (2, 2), (19, 0), (5, 4), (8, 2), (19, 1), (12, 1), (16, 1), (17, 2), (18, 2), (10, 3), (14, 3),
-    (17, 3), (18, 3), (17, 4), (18, 4), (6, 7), (20, 0), (19, 2), (6, 6), (8, 3), (7, 7), (7, 6), (2, 3), (17, 5),
-    (18, 5), (20, 2), (12, 3), (15, 3), (11, 2), (19, 4), (19, 3), (8, 4), (17, 6), (18, 6), (19, 5), (20, 1), (10,
-    4), (21, 2), (9, 3), (14, 4), (21, 0), (20, 4), (9, 2), (11, 3), (20, 3), (19, 6), (16, 2), (17, 7), (18, 7),
-    (20, 5), (5, 5), (8, 5), (21, 1), (21, 4), (16, 3), (20, 6), (19, 7), (17, 8), (18, 8), (12, 4), (15, 4), (11,
-    4), (5, 6), (21, 5), (21, 3), (21, 6), (10, 5), (20, 7), (14, 5), (19, 8), (8, 6), (9, 4), (16, 4), (17, 9),
-    (18, 9), (10, 6), (12, 5), (15, 5), (21, 7), (22, 4), (9, 6), (11, 5), (5, 7), (22, 5), (19, 9), (12, 6), (15,
-    6), (20, 8), (22, 1), (22, 0), (8, 7), (9, 5), (16, 5), (14, 6), (10, 7), (14, 7), (11, 6), (20, 9), (17, 10),
-    (18, 10), (21, 8), (12, 7), (15, 7), (11, 7), (22, 6), (21, 9), (16, 6), (17, 11), (18, 11), (19, 10), (9, 7),
-    (16, 7), (17, 12), (18, 12), (19, 11), (20, 10), (19, 12), (22, 2), (17, 13), (18, 13), (22, 3), (20, 11), (20,
-    12), (19, 13), (22, 8), (22, 9), (21, 10), (20, 13), (21, 12), (21, 11), (21, 13), (22, 7), (22, 12), (22, 10),
-    (22, 11), (22, 13),
+    (4, 0), (5, 0), (6, 0), (6, 2), (5, 1), (0, 0), (4, 1), (4, 2), (4, 3), (7, 0), (9, 0), (8, 0), (11, 2), (5, 3),
+    (4, 4), (5, 5), (4, 5), (4, 6), (4, 7), (11, 0), (1, 0), (7, 1), (10, 0), (6, 1), (12, 0), (8, 1), (2, 0), (3,
+    0), (13, 0), (8, 2), (5, 7), (14, 0), (10, 1), (9, 1), (7, 2), (7, 3), (5, 6), (13, 2), (5, 2), (5, 4), (11, 1),
+    (15, 2), (16, 2), (6, 3), (8, 3), (2, 1), (3, 1), (14, 1), (7, 4), (17, 0), (18, 0), (18, 1), (19, 0), (7, 5),
+    (19, 1), (12, 1), (8, 4), (8, 5), (2, 2), (3, 2), (20, 0), (6, 4), (9, 2), (20, 1), (13, 1), (17, 1), (18, 2),
+    (19, 2), (11, 3), (15, 3), (18, 3), (19, 3), (18, 4), (19, 4), (7, 7), (21, 0), (20, 2), (7, 6), (9, 3), (8, 7),
+    (8, 6), (2, 3), (3, 3), (18, 5), (19, 5), (21, 2), (13, 3), (16, 3), (12, 2), (20, 4), (20, 3), (9, 4), (18, 6),
+    (19, 6), (20, 5), (21, 1), (11, 4), (22, 2), (10, 3), (15, 4), (22, 0), (21, 4), (10, 2), (12, 3), (21, 3), (20,
+    6), (17, 2), (18, 7), (19, 7), (21, 5), (6, 5), (9, 5), (22, 1), (22, 4), (17, 3), (21, 6), (20, 7), (18, 8),
+    (19, 8), (13, 4), (16, 4), (12, 4), (6, 6), (22, 5), (22, 3), (22, 6), (11, 5), (21, 7), (15, 5), (20, 8), (9,
+    6), (10, 4), (17, 4), (18, 9), (19, 9), (11, 6), (13, 5), (16, 5), (22, 7), (23, 4), (10, 6), (12, 5), (6, 7),
+    (23, 5), (20, 9), (13, 6), (16, 6), (21, 8), (23, 1), (23, 0), (9, 7), (10, 5), (17, 5), (15, 6), (11, 7), (15,
+    7), (12, 6), (21, 9), (18, 10), (19, 10), (22, 8), (13, 7), (16, 7), (12, 7), (23, 6), (22, 9), (17, 6), (18,
+    11), (19, 11), (20, 10), (10, 7), (17, 7), (18, 12), (19, 12), (20, 11), (21, 10), (20, 12), (23, 2), (18, 13),
+    (19, 13), (23, 3), (21, 11), (21, 12), (20, 13), (23, 8), (23, 9), (22, 10), (21, 13), (22, 12), (22, 11), (22,
+    13), (23, 7), (23, 12), (23, 10), (23, 11), (23, 13),
 )
 
 
@@ -100,7 +103,9 @@
         )
 
     def send(kind, q, src, dst, to):
-        c = copy(kind, q, src, dst, to)
+        go(copy(kind, q, src, dst, to))
+
+    def go(c):
         c.start()
         sent.append(c)
 
@@ -121,19 +126,46 @@
     def piece(x, rel, q, size=1):
         return cols.at[x, at(4 * START[q] + rel * SIZES[q], size * SIZES[q])]
 
+    def away(kind, q):
+        src = raw.at[ylo, chunk_rows(1 - ylo, q)]
+        if kind == "oa":
+            return copy(kind, q, src, piece(x, ylo, q), to_yb)
+        return copy(kind, q, src, piece(x, 1 - ylo, q), to_yo)
+
     def send_yo(q):
-        send("ob", q, raw.at[ylo, chunk_rows(1 - ylo, q)], piece(x, 1 - ylo, q), to_yo)
+        if q not in EARLY:
+            go(away("ob", q))
 
     def send_yb(q):
-        send("oa", q, raw.at[ylo, chunk_rows(1 - ylo, q)], piece(x, ylo, q), to_yb)
+        if q not in EARLY:
+            go(away("oa", q))
         rows = raw.at[ylo, chunk_rows(ylo, q)]
         send("j0", q, rows, rows, to_yb)
 
-    def send_own(q):
+    def own_copies(q):
+        own = piece(x, 2, q)
+        return copy("xr0", q, own, own, to_xp), copy("xl0", q, own, own, to_xm)
+
+    def place_own(q):
         own = piece(x, 2, q)
         own[...] = raw[ylo, chunk_rows(ylo, q), :]
-        send("xr0", q, own, own, to_xp)
-        send("xl0", q, own, own, to_xm)
+
+    def send_own(q):
+        if q not in EARLY:
+            place_own(q)
+            for c in own_copies(q):
+                go(c)
+
+    def early_own():
+        for q in EARLY:
+            place_own(q)
+            for c in own_copies(q):
+                c.start()
+
+    def early_away():
+        for q in EARLY:
+            away("oa", q).start()
+            away("ob", q).start()
 
     def recv_next(q):
         arrived("oa", q, piece(x, 1 - ylo, q))
@@ -215,7 +247,6 @@
             send(f"row{2 * j + c}", None, raw.at[1 - ylo, rows], raw.at[1 - ylo, rows], sib)
 
     def rows_ready(j):
-        send_rows(j)
         if j == 0:
             for i, kind in enumerate(("m2a", "m2b", "m2c")):
                 arrived(kind, None, m2.at[i + 1])
@@ -347,23 +378,36 @@
     pl.semaphore_wait(barrier, len(peers))
     exchange("sib0", other)
     exchange("sib1", core)
+    mine = core == ylo
+    pl.when(mine)(early_own)
+    pl.when(jnp.logical_not(mine))(early_away)
     arrived("sib0", None, raw.at[ylo, at(other * UNIT + core * HALF, HALF)])
+    pl.when(mine)(early_away)
+    pl.when(jnp.logical_not(mine))(early_own)
+    for q in EARLY:
+        sent.extend(own_copies(q) + (away("oa", q), away("ob", q)))
 
     steps = (
-        lambda _: means1(), lambda _: means2(), rows_ready,
+        lambda _: means1(), lambda _: means2(), send_rows, rows_ready,
         send_yb, send_yo, send_own, recv_next, pass_far, send_next, send_far, forward_own, forward_next, end_own,
         forward_far, across1, across2, columns, product, reduce0, reduce1,
         lambda u: reduce_mid(u, 1), lambda u: reduce_mid(u, 2), reduce_end,
     )
+    done, marks = 0, []
     for step, index in ORDER:
+        marks.append(len(sent))
         steps[step](index)
+        if len(marks) > LAG:
+            for c in sent[done:marks[-LAG]]:
+                c.wait_send()
+            done = marks[-LAG]
     for u in range(len(PARTS)):
         arrived("fin", u, final(u, other))
     for j in range(GROUPS):
         turned = fin[j].T
         for h in range(2):
             out_ref[h * HALF + j * GROUP:h * HALF + (j + 1) * GROUP, :] = turned[h * GROUP:(h + 1) * GROUP]
-    for c in sent:
+    for c in sent[done:]:
         c.wait_send()
 
 

time: 144 us -> 141 us (0.979)
  Pallas kernels: 142 us -> 139 us
    pallas_call x1, Pallas kernels: 142 us -> 139 us  [shards(): pl.pallas_call(kernel, out_shape=jax.ShapeDtypeStruct((UNIT, UNIT), f32),...]
where the time goes in v3:
time: 141 us
  Pallas kernels  139 us (99%)
  local copies, waits for them, and re-layouts  2.26 us (2%)
    pallas_call x1, Pallas kernels, shards(): pl.pallas_call(kernel, out_shape=jax.ShapeDtypeStruct((UNIT, UNIT), f32),...  139 us

profile of v3, /device:TPU:1, one launch (start us, length us, event | category | flops | bytes accessed | tf_op | source)
XLA Modules:
  0.0 141.3 jit_solution(12693612848472288187)
XLA Ops:
  0.0 139.0 %shard_map.17 = f32[512,512]{1,0:T(8,128)} custom-call(f32[2,512,384]{2,1,0:T(8,128)} %in_ref.1), custom_call_target="tpu_custom_call" | custom-call | flops 20000000000 | bytes 4194304 | tf_op jit(solution)/shard_map/pallas_call | solution.py:426
  139.0 2.3 %copy.3 = f32[512,512]{1,0:T(8,128)} copy(f32[512,512]{1,0:T(8,128)} %shard_map.17) | data formatting | bytes 2097152

commit v4 on v3

--- a/solution.py
+++ b/solution.py
@@ -286,8 +286,7 @@
         q, j0, count = PARTS[u]
         keep, width = q % KEEP, 8 * SIZES[q]
 
-        @pl.loop(0, count * GROUP // 64)
-        def _(r):
+        def some(r):
             rows = pl.ds(pl.multiple_of(j0 * 4 * GROUP + r * HALF, HALF), HALF)
             n = GROUP // 64
             lanes = pl.ds(pl.multiple_of(lax.rem(r, n) * HALF, HALF), HALF)
@@ -295,6 +294,11 @@
             tile[j0 + lax.div(r, n), 8 * START[q]:8 * START[q] + width, lanes] = (
                 dot(ch, rh) + dot(ch, rlo[rows, :]) + dot(clo[keep, :width], rh)
             )
+
+        if count == 4:
+            pl.loop(0, 2)(lambda r: (some(2 * r), some(2 * r + 1)) and None)
+        else:
+            pl.loop(0, count * GROUP // 64)(some)
 
     def block(u, step, lanes=slice(None)):
         q, j0, count = PARTS[u]

time: 141 us -> 141 us (level)
  no operation moved by 1% of the time
where the time goes in v4:
time: 141 us
  Pallas kernels  139 us (99%)
  local copies, waits for them, and re-layouts  2.26 us (2%)
    pallas_call x1, Pallas kernels, shards(): pl.pallas_call(kernel, out_shape=jax.ShapeDtypeStruct((UNIT, UNIT), f32),...  139 us

profile of v4, /device:TPU:1, one launch (start us, length us, event | category | flops | bytes accessed | tf_op | source)
XLA Modules:
  0.0 141.3 jit_solution(13657892225030648295)
XLA Ops:
  0.0 139.0 %shard_map.17 = f32[512,512]{1,0:T(8,128)} custom-call(f32[2,512,384]{2,1,0:T(8,128)} %in_ref.1), custom_call_target="tpu_custom_call" | custom-call | flops 20000000000 | bytes 4194304 | tf_op jit(solution)/shard_map/pallas_call | solution.py:430
  139.0 2.3 %copy.3 = f32[512,512]{1,0:T(8,128)} copy(f32[512,512]{1,0:T(8,128)} %shard_map.17) | data formatting | bytes 2097152
